TPU v7x, 32 devices: a whole 2x2x4 slice. The times are simulated.
32 devices in a mesh: groups: 2 (over y), fsdp: 16 (over z, x, core).
Axes of the slice: x: 2, y: 2, z: 4, core: 2. Of those that a mesh axis runs over, the one named last changes fastest.
Arguments:
- grad_shards: bfloat16 [32, 512, 512], P('groups', 'fsdp'), parts along dimension 0, may hold values from -57 to 57
- offsets: int32 [32], P('groups'), parts along dimension 0, may hold values from 0 to 15, each once
- owners: int32 [32], P('groups'), parts along dimension 0, may hold values from 0 to 15, as said below
- left_stats: float32 [64, 512, 512], P(('groups', 'fsdp')), parts along dimension 0, may hold values from -0.4 to 8
- right_stats: float32 [64, 512, 512], P(('groups', 'fsdp')), parts along dimension 0, may hold values from -0.4 to 8
- left_root: bfloat16 [64, 512, 512], P(('groups', 'fsdp')), parts along dimension 0, may hold values from -0.11 to 1.21
- right_root: bfloat16 [64, 512, 512], P(('groups', 'fsdp')), parts along dimension 0, may hold values from -0.11 to 1.21
Outputs:
- update: bfloat16 [32, 512, 512], P('groups', 'fsdp'), parts along dimension 0
- new_left_stats: float32 [64, 512, 512], P(('groups', 'fsdp')), parts along dimension 0
- new_right_stats: float32 [64, 512, 512], P(('groups', 'fsdp')), parts along dimension 0
There are 2 independent parts, one for each index of `groups`. A program takes and returns all parts, laid end to end along the dimension named above; each array names one. Nothing has to cross between parts.
Inputs may be any that keep to these rules, and one draw needn't show every extreme that they name: `owners`: every owner is named by at most 2 blocks, and some owner by exactly 2. Owners 2 k and 2 k + 1 are named by 2 blocks together, for every k.
All inputs are finite; a program needn't handle non-finite values.
Results may differ from a plain program's by a relative error of at most 0.0049.
Values may be sent and summed in bfloat16 or wider, within the bound.
A program may use at most 64 MiB of HBM per device.

v0:
```python
import jax
import jax.numpy as jnp
from jax import lax
from jax.sharding import PartitionSpec as P

DECAY = 0.999
CLIP_RMS = 1.0
EPSILON = 1e-06


def slot_tables(owners, peer_count, capacity):
    block_count = owners.shape[0]
    block_ids = jnp.arange(block_count, dtype=jnp.int32)
    same_owner = owners[None, :] == owners[:, None]
    earlier = block_ids[None, :] < block_ids[:, None]
    slot_rank = jnp.sum((same_owner & earlier).astype(jnp.int32), axis=1)
    slot_ids = jnp.arange(capacity, dtype=jnp.int32)
    holder_ids = jnp.arange(peer_count, dtype=jnp.int32)
    slot_match = (owners[None, None, :] == holder_ids[None, :, None]) & (
        slot_rank[None, None, :] == slot_ids[:, None, None]
    )
    return (slot_rank, slot_match)


def precondition(gradient, grad_mean, left_old, right_old, left_inv, right_inv, clip_factor):
    left_new = DECAY * left_old + (1.0 - DECAY) * jnp.dot(
        gradient, gradient.T, preferred_element_type=jnp.float32
    )
    right_new = DECAY * right_old + (1.0 - DECAY) * jnp.dot(
        gradient.T, gradient, preferred_element_type=jnp.float32
    )
    left_half = jnp.dot(left_inv, gradient, preferred_element_type=jnp.float32).astype(jnp.bfloat16)
    direction = jnp.dot(left_half, right_inv, preferred_element_type=jnp.float32)
    graft_scale = jnp.sqrt(grad_mean / (jnp.mean(direction * direction) + EPSILON))
    return (left_new, right_new, (clip_factor * (graft_scale * direction)).astype(jnp.bfloat16))


def body(grad_shards, offsets, owners, left_stats, right_stats, left_root, right_root):
    peer_count = lax.axis_size("fsdp")
    capacity = left_stats.shape[0]
    block_count, strip_rows, block_size = grad_shards.shape
    slot_rank, slot_match = slot_tables(owners, peer_count, capacity)
    positions = jnp.arange(block_count, dtype=jnp.int32)
    at_position = (offsets[None, :] == positions[:, None]).astype(jnp.int32)
    matched = slot_match.astype(jnp.int32)
    source_rows = jnp.sum(matched * offsets[None, None, :], axis=2).reshape(-1)
    occupied = jnp.sum(matched, axis=2).reshape(-1)
    picked = jnp.take(grad_shards, source_rows, axis=0)
    picked = jnp.where(occupied[:, None, None] > 0, picked, jnp.zeros_like(picked))
    outgoing = picked.reshape(capacity, peer_count * strip_rows, block_size)
    arrived = lax.all_to_all(outgoing, "fsdp", split_axis=1, concat_axis=1, tiled=True)
    widened = arrived.astype(jnp.float32)
    slot_squares = jnp.sum(widened * widened, axis=(1, 2))
    entries = block_count * block_size * block_size
    local_grad = grad_shards.astype(jnp.float32)
    square_sum = lax.psum(jnp.sum(local_grad * local_grad), "fsdp")
    clip_factor = jnp.minimum(1.0, CLIP_RMS * lax.rsqrt(square_sum / entries))
    left_list = []
    right_list = []
    update_list = []
    for slot_index in range(capacity):
        grad_mean = slot_squares[slot_index] / (block_size * block_size)
        left_new, right_new, slot_update = precondition(
            arrived[slot_index],
            grad_mean,
            left_stats[slot_index],
            right_stats[slot_index],
            left_root[slot_index],
            right_root[slot_index],
            clip_factor,
        )
        left_list.append(left_new)
        right_list.append(right_new)
        update_list.append(slot_update)
    slot_updates = jnp.stack(update_list)
    returned = lax.all_to_all(slot_updates, "fsdp", split_axis=1, concat_axis=1, tiled=True)
    anchor = slot_rank * peer_count + owners
    where_from = jnp.sum(at_position * anchor[None, :], axis=1)
    update = jnp.take(
        returned.reshape(capacity * peer_count, strip_rows, block_size), where_from, axis=0
    )
    return (update, jnp.stack(left_list), jnp.stack(right_list))


def solution(mesh):
    placed = (
        P("groups", "fsdp", None),
        P("groups"),
        P("groups"),
        P(("groups", "fsdp"), None, None),
        P(("groups", "fsdp"), None, None),
        P(("groups", "fsdp"), None, None),
        P(("groups", "fsdp"), None, None),
    )
    return jax.shard_map(
        body,
        mesh=mesh,
        in_specs=placed,
        out_specs=(
            P("groups", "fsdp", None),
            P(("groups", "fsdp"), None, None),
            P(("groups", "fsdp"), None, None),
        ),
        check_vma=False,
    )
```

profile of v0, /device:TPU:1, one launch (start us, length us, event | category | flops | bytes accessed | tf_op | source)
XLA Modules:
  0.0 107.0 jit_solution(9946992853010153165)
XLA Ops:
  0.6 0.9 convert_reduce_fusion
  1.5 0.7 iota_compare_fusion
  2.2 0.8 fusion.25
  3.5 1.7 %gather_fusion = bf16[32,32,512]{2,1,0:T(8,128)(2,1)S(1)} fusion(bf16[16,32,512]{2,1,0:T(8,128)(2,1)} %param.7, s32[1024]{0:T(1024)S(1)} %pad_clamp_fusion.1), kind=kCustom, calls=%fused_computation | custom fusion | bytes 2097280 | tf_op jit(solution)/shard_map/jit(_take)/gather | solution.py:48
  5.6 2.0 %copy.19 = bf16[2,512,512]{2,0,1:T(2,128)(2,1)} copy(bf16[2,512,512]{2,1,0:T(8,128)(2,1)S(1)} %fusion.10) | data formatting | bytes 2097152 | tf_op jit(solution)/shard_map/jit(_where)/select_n | solution.py:49
  7.7 7.3 %all-to-all-start = ((bf16[2,512,512]{2,0,1:T(2,128)(2,1)}), bf16[2,512,512]{2,0,1:T(2,128)(2,1)S(1)}, u32[]{:S(2)}, u32[]{:S(2)}) async-start(bf16[2,512,512]{2,0,1:T(2,128)(2,1)} %copy.19), calls=%async_computation | async-start | bytes 2097152 | tf_op jit(solution)/shard_map/all_to_all | solution.py:51
  15.0 0.9 multiply_reduce_fusion.3
  15.9 44.2 %psum.7 = f32[]{:T(128)} all-reduce(f32[]{:T(128)} %multiply_reduce_fusion.3), channel_id=1, replica_groups=mesh['groups'=2,'fsdp'=16] {'fsdp'}, use_global_device_ids=true, to_apply=%region_3.4 | all-reduce | flops 1 | bytes 8 | tf_op jit(solution)/shard_map/psum | solution.py:56
  60.8 2.3 %multiply_reduce_fusion = f32[2]{0:T(128)S(1)} fusion(bf16[2,512,512]{2,0,1:T(2,128)(2,1)S(1)} %all-to-all-done), kind=kLoop, calls=%fused_computation.4 | loop fusion | flops 1572862 | bytes 1048584 | tf_op jit(solution)/shard_map/reduce_sum | solution.py:53
  63.0 0.6 fusion.31
  63.6 1.5 %fusion.30 = (bf16[1,512,512]{2,0,1:T(2,128)(2,1)S(1)}, bf16[1,512,512]{2,0,1:T(2,128)(2,1)S(1)}) fusion(bf16[2,512,512]{2,0,1:T(2,128)(2,1)S(1)} %all-to-all-done), kind=kLoop, calls=%fused_computation.65 | loop fusion | bytes 2097152 | tf_op jit(solution)/shard_map/slice | solution.py:64
  65.1 2.8 %multiply_reduce_fusion.2 = (f32[]{:T(128)}, f32[512,512]{1,0:T(8,128)S(1)}) fusion(bf16[2,512,512]{2,1,0:T(8,128)(2,1)} %param.13, bf16[2,512,512]{2,1,0:T(8,128)(2,1)} %param.12, bf16[1,512,512]{2,0,1:T(2,128)(2,1)S(1)} %get-tuple-element.5), kind=kOutput, calls=%fused_computation.27 | convolution fusion | flops 537657344 | bytes 2621444 | tf_op jit(solution)/shard_map/dot_general | solution.py:33
  69.3 3.7 %multiply_reduce_fusion.1 = (f32[]{:T(128)}, f32[512,512]{1,0:T(8,128)}) fusion(bf16[2,512,512]{2,1,0:T(8,128)(2,1)} %param.13, bf16[2,512,512]{2,1,0:T(8,128)(2,1)} %param.12, bf16[1,512,512]{2,0,1:T(2,128)(2,1)S(1)} %get-tuple-element.6), kind=kOutput, calls=%fused_computation.25 | convolution fusion | flops 537657344 | bytes 2621444 | tf_op jit(solution)/shard_map/dot_general | solution.py:33
  74.5 1.1 %copy-done.3 = f32[512,512]{1,0:T(8,128)S(1)} copy-done((f32[512,512]{1,0:T(8,128)S(1)}, f32[512,512]{1,0:T(8,128)}, u32[]{:S(2)}) %copy-start.3) | copy-done | bytes 1048600
  75.8 2.1 %copy.22 = bf16[2,512,512]{2,0,1:T(2,128)(2,1)} copy(bf16[2,512,512]{2,1,0:T(8,128)(2,1)S(1)} %pad_maximum_fusion.2) | data formatting | bytes 2097152 | tf_op jit(solution)/shard_map/stack | solution.py:75
  77.9 4.3 %all-to-all-start.1 = ((bf16[2,512,512]{2,0,1:T(2,128)(2,1)}), bf16[2,512,512]{2,0,1:T(2,128)(2,1)S(1)}, u32[]{:S(2)}, u32[]{:S(2)}) async-start(bf16[2,512,512]{2,0,1:T(2,128)(2,1)} %copy.22), calls=%async_computation.1 | async-start | bytes 2097152 | tf_op jit(solution)/shard_map/all_to_all | solution.py:76
  82.4 1.8 %fusion.5 = f32[1,512,512]{2,1,0:T(8,128)S(1)} fusion(f32[2,512,512]{2,1,0:T(8,128)} %param.10, bf16[1,512,512]{2,0,1:T(2,128)(2,1)S(1)} %get-tuple-element.6), kind=kOutput, calls=%fused_computation.13 | convolution fusion | flops 269221888 | bytes 2621440 | tf_op jit(solution)/shard_map/dot_general | solution.py:26
  84.2 0.5 fusion.7
  84.7 1.5 %pad_maximum_fusion = f32[2,512,512]{2,1,0:T(8,128)} fusion(f32[1,512,512]{2,1,0:T(8,128)S(1)} %fusion.5, f32[1,512,512]{2,1,0:T(8,128)S(1)} %fusion.7), kind=kLoop, calls=%fused_computation.2 | loop fusion | flops 524288 | bytes 4194304 | tf_op jit(solution)/shard_map/stack | solution.py:82
  86.2 0.8 copy-done.2
  88.0 1.5 %pad_maximum_fusion.1 = f32[2,512,512]{2,1,0:T(8,128)} fusion(f32[1,512,512]{2,1,0:T(8,128)S(1)} %fusion.1, f32[1,512,512]{2,1,0:T(8,128)S(1)} %fusion.3), kind=kLoop, calls=%fused_computation.3 | loop fusion | flops 524288 | bytes 4194304 | tf_op jit(solution)/shard_map/stack | solution.py:82
  89.6 15.8 %all-to-all-done.1 = bf16[2,512,512]{2,0,1:T(2,128)(2,1)S(1)} async-done(((bf16[2,512,512]{2,0,1:T(2,128)(2,1)}), bf16[2,512,512]{2,0,1:T(2,128)(2,1)S(1)}, u32[]{:S(2)}, u32[]{:S(2)}) %all-to-all-start.1) | async-done | bytes 1048608 | tf_op jit(solution)/shard_map/all_to_all | solution.py:76
  105.5 0.6 gather_fusion.1
  106.1 0.9 broadcast_select_fusion
  (32 shorter events, 2.6 us)
Async XLA Ops:
  5.6 9.4 %copy-start = (bf16[16,32,512]{2,1,0:T(8,128)(2,1)S(1)}, bf16[16,32,512]{2,1,0:T(8,128)(2,1)}, u32[]{:S(2)}) copy-start(bf16[16,32,512]{2,1,0:T(8,128)(2,1)} %param.7) | copy-start | bytes 1572868
  7.7 53.1 %all-to-all-start = ((bf16[2,512,512]{2,0,1:T(2,128)(2,1)}), bf16[2,512,512]{2,0,1:T(2,128)(2,1)S(1)}, u32[]{:S(2)}, u32[]{:S(2)}) async-start(bf16[2,512,512]{2,0,1:T(2,128)(2,1)} %copy.19), calls=%async_computation | async-start | bytes 2097152 | tf_op jit(solution)/shard_map/all_to_all | solution.py:51
  74.3 1.2 %copy-start.3 = (f32[512,512]{1,0:T(8,128)S(1)}, f32[512,512]{1,0:T(8,128)}, u32[]{:S(2)}) copy-start(f32[512,512]{1,0:T(8,128)} %get-tuple-element.10) | copy-start | bytes 3145732
  75.8 6.4 %copy-start.4 = (s32[16]{0:T(128)S(1)}, s32[16]{0:T(128)}, u32[]{:S(2)}) copy-start(s32[16]{0:T(128)} %param.9) | copy-start | bytes 196
  75.8 6.4 %copy-start.5 = (s32[16]{0:T(128)S(1)}, s32[16]{0:T(128)}, u32[]{:S(2)}) copy-start(s32[16]{0:T(128)} %param.8) | copy-start | bytes 196
  77.9 27.5 %all-to-all-start.1 = ((bf16[2,512,512]{2,0,1:T(2,128)(2,1)}), bf16[2,512,512]{2,0,1:T(2,128)(2,1)S(1)}, u32[]{:S(2)}, u32[]{:S(2)}) async-start(bf16[2,512,512]{2,0,1:T(2,128)(2,1)} %copy.22), calls=%async_computation.1 | async-start | bytes 2097152 | tf_op jit(solution)/shard_map/all_to_all | solution.py:76
  82.2 2.0 %copy-start.1 = (f32[2,512,512]{2,1,0:T(8,128)S(1)}, f32[2,512,512]{2,1,0:T(8,128)}, u32[]{:S(2)}) copy-start(f32[2,512,512]{2,1,0:T(8,128)} %param.10) | copy-start | bytes 6291460
  84.7 2.4 %copy-start.2 = (f32[2,512,512]{2,1,0:T(8,128)S(1)}, f32[2,512,512]{2,1,0:T(8,128)}, u32[]{:S(2)}) copy-start(f32[2,512,512]{2,1,0:T(8,128)} %param.11) | copy-start | bytes 6291460
where the time goes:
time: 109 us; the launch traced here: 107 us
  blocking collectives  44.2 us (41%)
  waiting for transfers between devices  15.8 us (14%)
  starting transfers between devices  11.6 us (11%)
  local copies, waits for them, and re-layouts  11 us (10%)
  other arithmetic  10.4 us (10%)
  matrix products  9.76 us (9%)
  between operations  4.29 us (4%)
    psum x1, blocking collectives, body(): square_sum = lax.psum(jnp.sum(local_grad * local_grad), 'fsdp')  44.2 us
    all_to_all x1, waiting for transfers between devices, body(): lax.all_to_all(slot_updates, 'fsdp', split_axis=1, concat_axis=1, tiled=T...  15.8 us
    all_to_all x1, starting transfers between devices, body(): lax.all_to_all(outgoing, 'fsdp', split_axis=1, concat_axis=1, tiled=True)  7.32 us
    dot_general x2, matrix products, precondition(): jnp.dot(left_half, right_inv, preferred_element_type=jnp.float32)  6.48 us
    all_to_all x1, starting transfers between devices, body(): lax.all_to_all(slot_updates, 'fsdp', split_axis=1, concat_axis=1, tiled=T...  4.27 us
    another operation x2, other arithmetic, body(): return (update, jnp.stack(left_list), jnp.stack(right_list))  3.03 us
    dot_general x2, matrix products, precondition(): jnp.dot(gradient, gradient.T, preferred_element_type=jnp.float32)  2.32 us
    reduce_sum x1, other arithmetic, body(): slot_squares = jnp.sum(widened * widened, axis=(1, 2))  2.27 us
  transfers between devices with their start and end apart: 2, of which 1 were waited for; matrix products, arithmetic and copies ran while one was open for 7% of the time, Pallas kernels for 0%

commit v1 on v0

--- a/solution.py
+++ b/solution.py
@@ -1,6 +1,10 @@
+import functools
+
 import jax
 import jax.numpy as jnp
 from jax import lax
+from jax.experimental import pallas as pl
+from jax.experimental.pallas import tpu as pltpu
 from jax.sharding import PartitionSpec as P
 
 DECAY = 0.999
@@ -35,7 +39,7 @@
     return (left_new, right_new, (clip_factor * (graft_scale * direction)).astype(jnp.bfloat16))
 
 
-def body(grad_shards, offsets, owners, left_stats, right_stats, left_root, right_root):
+def padded_body(grad_shards, offsets, owners, left_stats, right_stats, left_root, right_root):
     peer_count = lax.axis_size("fsdp")
     capacity = left_stats.shape[0]
     block_count, strip_rows, block_size = grad_shards.shape
@@ -82,6 +86,325 @@
     return (update, jnp.stack(left_list), jnp.stack(right_list))
 
 
+AXIS = "fsdp"
+MESH = pl.DeviceIdType.MESH
+
+
+def exchange_kernel(
+    n,
+    offsets_ref,
+    owners_ref,
+    grad_hbm,
+    left_hbm,
+    right_hbm,
+    returned_ref,
+    slot_grad_ref,
+    table_ref,
+    grad_ref,
+    outgoing_ref,
+    blocks_ref,
+    left_ref,
+    right_ref,
+    update_ref,
+    sums_ref,
+    local_sem,
+    strip_send,
+    strip_recv,
+    sum_send,
+    sum_recv,
+    back_send,
+    back_recv,
+    pair_send,
+    pair_recv,
+):
+    strip = grad_ref.shape[1]
+    block_size = grad_ref.shape[2]
+    capacity = left_hbm.shape[0]
+    me = lax.axis_index(AXIS)
+    side = lax.rem(me, 2)
+    pair = me // 2
+    sibling = me + 1 - 2 * side
+
+    def peer(step):
+        return lax.rem(me + lax.rem(step * 7, n), n)
+
+    def rows_of(device):
+        return pl.ds(pl.multiple_of(device * strip, strip), strip)
+
+    def strip_copy(source, target):
+        return pltpu.make_async_remote_copy(
+            src_ref=outgoing_ref.at[target],
+            dst_ref=blocks_ref.at[lax.rem(target, 2), rows_of(source)],
+            send_sem=strip_send.at[target],
+            recv_sem=strip_recv.at[source],
+            device_id={AXIS: target},
+            device_id_type=MESH,
+        )
+
+    def sum_copy(source, target):
+        return pltpu.make_async_remote_copy(
+            src_ref=sums_ref.at[source],
+            dst_ref=sums_ref.at[source],
+            send_sem=sum_send.at[target],
+            recv_sem=sum_recv.at[source],
+            device_id={AXIS: target},
+            device_id_type=MESH,
+        )
+
+    def back_copy(source, target):
+        return pltpu.make_async_remote_copy(
+            src_ref=update_ref.at[rows_of(target)],
+            dst_ref=returned_ref.at[source],
+            send_sem=back_send.at[target],
+            recv_sem=back_recv.at[source],
+            device_id={AXIS: target},
+            device_id_type=MESH,
+        )
+
+    def pair_copy(index, source, target):
+        return pltpu.make_async_remote_copy(
+            src_ref=source,
+            dst_ref=target,
+            send_sem=pair_send.at[index],
+            recv_sem=pair_recv.at[index],
+            device_id={AXIS: sibling},
+            device_id_type=MESH,
+        )
+
+    def each_peer(action):
+        def step(index, carry):
+            action(peer(index))
+            return carry
+
+        lax.fori_loop(1, n, step, 0)
+
+    barrier = pltpu.get_barrier_semaphore()
+    each_peer(
+        lambda other: pl.semaphore_signal(
+            barrier, inc=1, device_id={AXIS: other}, device_id_type=MESH
+        )
+    )
+    own_slots = pl.ds(side * capacity, capacity)
+    other_slots = pl.ds((1 - side) * capacity, capacity)
+    grad_load = pltpu.make_async_copy(grad_hbm, grad_ref, local_sem.at[0])
+    left_load = pltpu.make_async_copy(left_hbm, left_ref.at[own_slots], local_sem.at[1])
+    right_load = pltpu.make_async_copy(right_hbm, right_ref.at[own_slots], local_sem.at[2])
+    grad_load.start()
+    left_load.start()
+    right_load.start()
+
+    owners = [owners_ref[b] for b in range(n)]
+    offsets = [offsets_ref[b] for b in range(n)]
+    pairs = [owner // 2 for owner in owners]
+    for k in range(n // 2):
+        first = offsets[0]
+        last = offsets[0]
+        for b in range(1, n):
+            last = jnp.where(pairs[b] == k, offsets[b], last)
+        for b in range(n - 1, -1, -1):
+            first = jnp.where(pairs[b] == k, offsets[b], first)
+        table_ref[2 * k] = first
+        table_ref[2 * k + 1] = last
+    first_owner = owners[0]
+    last_owner = owners[0]
+    for b in range(1, n):
+        last_owner = jnp.where(pairs[b] == pair, owners[b], last_owner)
+    for b in range(n - 1, -1, -1):
+        first_owner = jnp.where(pairs[b] == pair, owners[b], first_owner)
+    same = first_owner == last_owner
+    first_side = lax.rem(first_owner, 2)
+    last_side = lax.rem(last_owner, 2)
+    last_rank = jnp.where(same, 1, 0)
+    chosen = jnp.where(side == 0, first_side * capacity, last_side * capacity + last_rank)
+
+    grad_load.wait()
+    pl.semaphore_wait(barrier, n - 1)
+
+    def send_strip(other):
+        outgoing_ref[other] = grad_ref[table_ref[other]]
+        strip_copy(me, other).start()
+
+    each_peer(send_strip)
+
+    squares = jnp.zeros((strip, block_size), jnp.float32)
+    for b in range(n):
+        wide = grad_ref[b].astype(jnp.float32)
+        squares += wide * wide
+    partial = squares[0:8]
+    for r in range(8, strip, 8):
+        partial += squares[r : r + 8]
+    lanes = partial[:, 0:128]
+    for c in range(128, block_size, 128):
+        lanes += partial[:, c : c + 128]
+    sums_ref[me] = lanes
+    each_peer(lambda other: sum_copy(me, other).start())
+
+    left_swap = pair_copy(0, left_hbm, left_ref.at[own_slots])
+    right_swap = pair_copy(1, right_hbm, right_ref.at[own_slots])
+    left_swap.start()
+    right_swap.start()
+    blocks_ref[side, rows_of(me)] = grad_ref[table_ref[me]]
+
+    each_peer(lambda other: sum_copy(other, me).wait_recv())
+    total = jnp.sum(jnp.sum(sums_ref[...], axis=0), axis=(0, 1), keepdims=True)
+    entries = n * block_size * block_size
+    clip_factor = jnp.minimum(1.0, CLIP_RMS * lax.rsqrt(total / entries))
+    left_load.wait()
+    right_load.wait()
+    pair_copy(0, left_hbm, left_ref.at[other_slots]).wait_recv()
+    pair_copy(1, right_hbm, right_ref.at[other_slots]).wait_recv()
+
+    each_peer(lambda other: strip_copy(other, me).wait_recv())
+    block_swap = pair_copy(2, blocks_ref.at[side], blocks_ref.at[side])
+    block_swap.start()
+
+    block = blocks_ref[side]
+    wide = block.astype(jnp.float32)
+    grad_mean = jnp.sum(wide * wide, axis=(0, 1), keepdims=True) / (block_size * block_size)
+    left_half = jnp.dot(left_ref[chosen], block, preferred_element_type=jnp.float32)
+    direction = jnp.dot(
+        left_half.astype(jnp.bfloat16), right_ref[chosen], preferred_element_type=jnp.float32
+    )
+    direction_mean = jnp.sum(direction * direction, axis=(0, 1), keepdims=True) / (
+        block_size * block_size
+    )
+    graft_scale = jnp.sqrt(grad_mean / (direction_mean + EPSILON))
+    update_ref[...] = (clip_factor * (graft_scale * direction)).astype(jnp.bfloat16)
+    each_peer(lambda other: back_copy(me, other).start())
+    returned_ref[me] = update_ref[rows_of(me)]
+
+    pair_copy(2, blocks_ref.at[1 - side], blocks_ref.at[1 - side]).wait_recv()
+    for s in range(capacity):
+        from_first = (first_side == side) & (s == 0)
+        from_last = (last_side == side) & (last_rank == s)
+        index = jnp.where(from_last, 1, 0)
+        filled = jnp.where(from_first | from_last, 1.0, 0.0).astype(jnp.bfloat16)
+        slot_grad_ref[s] = blocks_ref[index] * filled
+
+    left_swap.wait_send()
+    right_swap.wait_send()
+    block_swap.wait_send()
+    each_peer(lambda other: strip_copy(me, other).wait_send())
+    each_peer(lambda other: sum_copy(me, other).wait_send())
+    each_peer(lambda other: back_copy(other, me).wait_recv())
+    each_peer(lambda other: back_copy(me, other).wait_send())
+
+
+def exchange(n, grad_shards, offsets, owners, left_root, right_root):
+    blocks, strip, size = grad_shards.shape
+    capacity = left_root.shape[0]
+    half = jnp.bfloat16
+    vmem = pl.BlockSpec(memory_space=pltpu.VMEM)
+    smem = pl.BlockSpec(memory_space=pltpu.SMEM)
+    anywhere = pl.BlockSpec(memory_space=pl.ANY)
+    many = pltpu.SemaphoreType.DMA((n,))
+    few = pltpu.SemaphoreType.DMA((3,))
+    return pl.pallas_call(
+        functools.partial(exchange_kernel, n),
+        out_shape=(
+            jax.ShapeDtypeStruct((n, strip, size), half),
+            jax.ShapeDtypeStruct((capacity, size, size), half),
+            jax.ShapeDtypeStruct((n,), jnp.int32),
+        ),
+        in_specs=[smem, smem, anywhere, anywhere, anywhere],
+        out_specs=(vmem, vmem, smem),
+        scratch_shapes=[
+            pltpu.VMEM((blocks, strip, size), half),
+            pltpu.VMEM((n, strip, size), half),
+            pltpu.VMEM((2, size, size), half),
+            pltpu.VMEM((2 * capacity, size, size), half),
+            pltpu.VMEM((2 * capacity, size, size), half),
+            pltpu.VMEM((size, size), half),
+            pltpu.VMEM((n, 8, 128), jnp.float32),
+            few,
+            many,
+            many,
+            many,
+            many,
+            many,
+            many,
+            few,
+            few,
+        ],
+        compiler_params=pltpu.CompilerParams(
+            collective_id=0, has_side_effects=True, vmem_limit_bytes=24 * 1024 * 1024
+        ),
+        cost_estimate=pl.CostEstimate(
+            flops=4 * size**3, bytes_accessed=100 * 1024 * 1024, transcendentals=0
+        ),
+        name="exchange",
+    )(offsets, owners, grad_shards, left_root, right_root)
+
+
+def statistics_kernel(
+    table_ref, returned_ref, slot_ref, left_ref, right_ref, update_ref, left_out, right_out
+):
+    tile = left_ref.shape[1]
+    part = pl.program_id(1)
+
+    @pl.when((pl.program_id(0) == 0) & (part == 0))
+    def _():
+        for d in range(returned_ref.shape[0]):
+            update_ref[table_ref[d]] = returned_ref[d]
+
+    span = pl.ds(pl.multiple_of(part * tile, tile), tile)
+    gradient = slot_ref[0]
+    rows = slot_ref[0, span, :]
+    columns = slot_ref[0, :, span]
+    left_out[0] = DECAY * left_ref[0] + (1.0 - DECAY) * lax.dot_general(
+        rows, gradient, (((1,), (1,)), ((), ())), preferred_element_type=jnp.float32
+    )
+    right_out[0] = DECAY * right_ref[0] + (1.0 - DECAY) * lax.dot_general(
+        columns, gradient, (((0,), (0,)), ((), ())), preferred_element_type=jnp.float32
+    )
+
+
+def statistics(table, returned, slot_grad, left_stats, right_stats):
+    capacity, size, _ = left_stats.shape
+    tile = size // 2
+    whole = pl.BlockSpec(returned.shape, lambda s, p, t: (0, 0, 0))
+    tiled = pl.BlockSpec((1, tile, size), lambda s, p, t: (s, p, 0))
+    return pl.pallas_call(
+        statistics_kernel,
+        grid_spec=pltpu.PrefetchScalarGridSpec(
+            num_scalar_prefetch=1,
+            grid=(capacity, size // tile),
+            in_specs=[
+                whole,
+                pl.BlockSpec((1, size, size), lambda s, p, t: (s, 0, 0)),
+                tiled,
+                tiled,
+            ],
+            out_specs=[whole, tiled, tiled],
+        ),
+        out_shape=(
+            jax.ShapeDtypeStruct(returned.shape, returned.dtype),
+            jax.ShapeDtypeStruct(left_stats.shape, jnp.float32),
+            jax.ShapeDtypeStruct(right_stats.shape, jnp.float32),
+        ),
+        compiler_params=pltpu.CompilerParams(vmem_limit_bytes=24 * 1024 * 1024),
+        cost_estimate=pl.CostEstimate(
+            flops=4 * capacity * size**3,
+            bytes_accessed=16 * capacity * size * size,
+            transcendentals=0,
+        ),
+        name="statistics",
+    )(table, returned, slot_grad, left_stats, right_stats)
+
+
+def body(grad_shards, offsets, owners, left_stats, right_stats, left_root, right_root):
+    n = lax.axis_size(AXIS)
+    blocks, strip, _ = grad_shards.shape
+    if blocks != n or strip % 16 or left_stats.shape[0] != 2:
+        return padded_body(
+            grad_shards, offsets, owners, left_stats, right_stats, left_root, right_root
+        )
+    returned, slot_grad, table = exchange(
+        n, grad_shards, offsets, owners, left_root, right_root
+    )
+    return statistics(table, returned, slot_grad, left_stats, right_stats)
+
+
 def solution(mesh):
     placed = (
         P("groups", "fsdp", None),

time: 109 us -> 48.1 us (0.44); the launches traced: 107 us -> 47.8 us
  blocking collectives: 44.2 us -> 0 us
  Pallas kernels: 0 us -> 40.6 us
  waiting for transfers between devices: 15.8 us -> 0 us
  starting transfers between devices: 11.6 us -> 0 us
  other arithmetic: 10.4 us -> 0 us
  matrix products: 9.76 us -> 0 us
  local copies, waits for them, and re-layouts: 11 us -> 6.53 us
  between operations: 4.29 us -> 0.68 us
    psum x1 -> x0, blocking collectives: 44.2 us -> none  [body(): square_sum = lax.psum(jnp.sum(local_grad * local_grad), 'fsdp')]
    pallas_call x0 -> x2, Pallas kernels: none -> 40.6 us  [the longest x1 36.9 us: exchange(): pl.pallas_call(functools.partial(exchange_kernel, n), out_shape=(jax.Shap...]
    all_to_all x2 -> x0, waiting for transfers between devices: 15.8 us -> none  [the longest x1 15.8 us: body(): lax.all_to_all(slot_updates, 'fsdp', split_axis=1, concat_axis=1, tiled=T...]
    all_to_all x2 -> x0, starting transfers between devices: 11.6 us -> none  [the longest x1 7.32 us: body(): lax.all_to_all(outgoing, 'fsdp', split_axis=1, concat_axis=1, tiled=True)]
    dot_general x6 -> x0, matrix products: 9.76 us -> none  [the longest x2 6.48 us: precondition(): jnp.dot(left_half, right_inv, preferred_element_type=jnp.float32)]
    reduce_sum x5 -> x0, other arithmetic: 4.97 us -> none  [the longest x1 2.27 us: body(): slot_squares = jnp.sum(widened * widened, axis=(1, 2))]
    unnamed x12 -> x14, local copies, waits for them, and re-layouts: 1.96 us -> 6.53 us
    another operation x5 -> x0, other arithmetic: 3.39 us -> none  [the longest x2 3.03 us: body(): return (update, jnp.stack(left_list), jnp.stack(right_list))]
  transfers between devices with their start and end apart: 2 -> 0, of which waited for: 1 -> 0; matrix products, arithmetic and copies ran while one was open for 7% -> 0% of each run, Pallas kernels for 0% -> 0%
where the time goes in v1:
time: 48.1 us; the launch traced here: 47.8 us
  Pallas kernels  40.6 us (84%)
  local copies, waits for them, and re-layouts  6.53 us (14%)
  between operations  0.68 us (1%)
    pallas_call x1, Pallas kernels, exchange(): pl.pallas_call(functools.partial(exchange_kernel, n), out_shape=(jax.Shap...  36.9 us
    unnamed x14, local copies, waits for them, and re-layouts  6.53 us
    pallas_call x1, Pallas kernels, statistics(): pl.pallas_call(statistics_kernel, grid_spec=pltpu.PrefetchScalarGridSpec(...  3.75 us

profile of v1, /device:TPU:1, one launch (start us, length us, event | category | flops | bytes accessed | tf_op | source)
XLA Modules:
  0.0 47.8 jit_solution(8743426838466943344)
XLA Ops:
  0.6 0.0 copy-start
  0.6 0.0 copy-start.2
  0.7 1.4 %copy-done.2 = bf16[2,512,512]{2,1,0:T(8,128)(2,1)S(1)} copy-done((bf16[2,512,512]{2,1,0:T(8,128)(2,1)S(1)}, bf16[2,512,512]{2,1,0:T(8,128)(2,1)}, u32[]{:S(2)}) %copy-start.2) | copy-done | bytes 1048600
  2.0 0.0 copy-start.3
  2.0 1.2 %copy-done.3 = bf16[2,512,512]{2,1,0:T(8,128)(2,1)S(1)} copy-done((bf16[2,512,512]{2,1,0:T(8,128)(2,1)S(1)}, bf16[2,512,512]{2,1,0:T(8,128)(2,1)}, u32[]{:S(2)}) %copy-start.3) | copy-done | bytes 1048600
  3.2 0.0 copy-start.4
  3.2 1.0 %copy-done.4 = bf16[16,32,512]{2,1,0:T(8,128)(2,1)S(1)} copy-done((bf16[16,32,512]{2,1,0:T(8,128)(2,1)S(1)}, bf16[16,32,512]{2,1,0:T(8,128)(2,1)}, u32[]{:S(2)}) %copy-start.4) | copy-done | bytes 524312
  4.3 0.0 copy-start.5
  4.3 0.7 %copy-done.5 = s32[16]{0:T(128)S(1)} copy-done((s32[16]{0:T(128)S(1)}, s32[16]{0:T(128)}, u32[]{:S(2)}) %copy-start.5) | copy-done | bytes 88
  4.9 0.0 copy-start.6
  4.9 0.7 %copy-done.6 = s32[16]{0:T(128)S(1)} copy-done((s32[16]{0:T(128)S(1)}, s32[16]{0:T(128)}, u32[]{:S(2)}) %copy-start.6) | copy-done | bytes 88
  5.6 36.9 %exchange.1 = (bf16[16,32,512]{2,1,0:T(8,128)(2,1)S(1)}, bf16[2,512,512]{2,1,0:T(8,128)(2,1)S(1)}, s32[16]{0:T(128)S(1)}) custom-call(s32[16]{0:T(128)S(1)} %copy-done.5, s32[16]{0:T(128)S(1)} %copy-done.6, bf16[16,32,512]{2,1,0:T(8,128)(2,1)S(1)} %copy-done.4, bf16[2,512,512]{2,1,0:T(8,128)(2,1)S(1)} %copy-done.2, bf16[2,512,512]{2,1,0:T(8,128)(2,1)S(1)} %copy-done.3), custom_call_target="tpu_custom_call" | custom-call | flops 536870912 | bytes 104857600 | tf_op jit(solution)/shard_map/exchange/pallas_call | solution.py:302
  42.5 0.0 copy-done
  42.5 0.0 copy-start.1
  42.5 1.6 %copy-done.1 = f32[2,512,512]{2,1,0:T(8,128)S(1)} copy-done((f32[2,512,512]{2,1,0:T(8,128)S(1)}, f32[2,512,512]{2,1,0:T(8,128)}, u32[]{:S(2)}) %copy-start.1) | copy-done | bytes 2097176
  44.1 3.8 %statistics.1 = (bf16[16,32,512]{2,1,0:T(8,128)(2,1)}, f32[2,512,512]{2,1,0:T(8,128)}, f32[2,512,512]{2,1,0:T(8,128)}) custom-call(s32[16]{0:T(128)S(1)} %get-tuple-element.6.table_ref, bf16[16,32,512]{2,1,0:T(8,128)(2,1)S(1)} %get-tuple-element.7.returned_ref, bf16[2,512,512]{2,1,0:T(8,128)(2,1)S(1)} %get-tuple-element.8.slot_ref, ...), custom_call_target="tpu_custom_call" | custom-call | flops 1073741824 | bytes 8388608 | tf_op jit(solution)/shard_map/statistics/pallas_call | solution.py:367
Async XLA Ops:
  0.6 41.8 %copy-start = (f32[2,512,512]{2,1,0:T(8,128)S(1)}, f32[2,512,512]{2,1,0:T(8,128)}, u32[]{:S(2)}) copy-start(f32[2,512,512]{2,1,0:T(8,128)} %left_ref.1) | copy-start | bytes 6291460
  0.6 1.4 %copy-start.2 = (bf16[2,512,512]{2,1,0:T(8,128)(2,1)S(1)}, bf16[2,512,512]{2,1,0:T(8,128)(2,1)}, u32[]{:S(2)}) copy-start(bf16[2,512,512]{2,1,0:T(8,128)(2,1)} %left_hbm.1) | copy-start | bytes 3145732
  2.0 1.2 %copy-start.3 = (bf16[2,512,512]{2,1,0:T(8,128)(2,1)S(1)}, bf16[2,512,512]{2,1,0:T(8,128)(2,1)}, u32[]{:S(2)}) copy-start(bf16[2,512,512]{2,1,0:T(8,128)(2,1)} %right_hbm.1) | copy-start | bytes 3145732
  3.2 1.0 %copy-start.4 = (bf16[16,32,512]{2,1,0:T(8,128)(2,1)S(1)}, bf16[16,32,512]{2,1,0:T(8,128)(2,1)}, u32[]{:S(2)}) copy-start(bf16[16,32,512]{2,1,0:T(8,128)(2,1)} %grad_hbm.1) | copy-start | bytes 1572868
  4.3 0.7 %copy-start.5 = (s32[16]{0:T(128)S(1)}, s32[16]{0:T(128)}, u32[]{:S(2)}) copy-start(s32[16]{0:T(128)} %offsets_ref.1) | copy-start | bytes 196
  4.9 0.7 %copy-start.6 = (s32[16]{0:T(128)S(1)}, s32[16]{0:T(128)}, u32[]{:S(2)}) copy-start(s32[16]{0:T(128)} %owners_ref.1) | copy-start | bytes 196
  42.5 1.6 %copy-start.1 = (f32[2,512,512]{2,1,0:T(8,128)S(1)}, f32[2,512,512]{2,1,0:T(8,128)}, u32[]{:S(2)}) copy-start(f32[2,512,512]{2,1,0:T(8,128)} %right_ref.1) | copy-start | bytes 6291460

commit v2 on v0

--- a/solution.py
+++ b/solution.py
@@ -1,6 +1,10 @@
+import functools
+
 import jax
 import jax.numpy as jnp
 from jax import lax
+from jax.experimental import pallas as pl
+from jax.experimental.pallas import tpu as pltpu
 from jax.sharding import PartitionSpec as P
 
 DECAY = 0.999
@@ -35,7 +39,7 @@
     return (left_new, right_new, (clip_factor * (graft_scale * direction)).astype(jnp.bfloat16))
 
 
-def body(grad_shards, offsets, owners, left_stats, right_stats, left_root, right_root):
+def padded_body(grad_shards, offsets, owners, left_stats, right_stats, left_root, right_root):
     peer_count = lax.axis_size("fsdp")
     capacity = left_stats.shape[0]
     block_count, strip_rows, block_size = grad_shards.shape
@@ -82,6 +86,387 @@
     return (update, jnp.stack(left_list), jnp.stack(right_list))
 
 
+AXIS = "fsdp"
+MESH = pl.DeviceIdType.MESH
+
+
+def mean_square(values):
+    return jnp.sum(values * values, axis=(0, 1), keepdims=True) / values.size
+
+
+def exchange_kernel(
+    n,
+    offsets_hbm,
+    owners_hbm,
+    grad_hbm,
+    left_hbm,
+    right_hbm,
+    left_root_hbm,
+    right_root_hbm,
+    update_ref,
+    left_out,
+    right_out,
+    offsets_ref,
+    owners_ref,
+    table_ref,
+    place_ref,
+    grad_ref,
+    outgoing_ref,
+    blocks_ref,
+    left_root_ref,
+    right_root_ref,
+    root_out_ref,
+    root_in_ref,
+    root_ref,
+    slot_update_ref,
+    returned_ref,
+    slot_grad_ref,
+    left_ref,
+    right_ref,
+    sums_ref,
+    local_sem,
+    stat_sem,
+    strip_send,
+    strip_recv,
+    sum_send,
+    sum_recv,
+    back_send,
+    back_recv,
+    pair_send,
+    pair_recv,
+):
+    strip, block_size = grad_ref.shape[1:]
+    capacity = left_root_hbm.shape[0]
+    pair_count = n // 2
+    me = lax.axis_index(AXIS)
+    pair = me // 2
+    side = me - 2 * pair
+    sibling = me + 1 - 2 * side
+
+    def wrapped(k):
+        ahead = pair + k
+        return jnp.where(ahead >= pair_count, ahead - pair_count, ahead)
+
+    middle = pair_count // 2
+    steps = sorted(range(1, pair_count), key=lambda k: (abs(k - middle), k))
+    to_first = [2 * wrapped(k) for k in steps]
+    to_last = [2 * wrapped(k) + 1 for k in steps]
+    others = to_first + to_last + [sibling]
+
+    def rows_of(device):
+        return pl.ds(pl.multiple_of(device * strip, strip), strip)
+
+    def remote(source, target, send_sem, recv_sem, device):
+        return pltpu.make_async_remote_copy(
+            src_ref=source,
+            dst_ref=target,
+            send_sem=send_sem,
+            recv_sem=recv_sem,
+            device_id={AXIS: device},
+            device_id_type=MESH,
+        )
+
+    def strip_copy(source, target):
+        return remote(
+            outgoing_ref.at[target],
+            blocks_ref.at[target - 2 * (target // 2), rows_of(source)],
+            strip_send.at[target],
+            strip_recv.at[source],
+            target,
+        )
+
+    def sum_copy(source, target):
+        row = sums_ref.at[source]
+        return remote(row, row, sum_send.at[target], sum_recv.at[source], target)
+
+    def back_copy(source, target):
+        return remote(
+            slot_update_ref.at[rows_of(target)],
+            returned_ref.at[source],
+            back_send.at[target],
+            back_recv.at[source],
+            target,
+        )
+
+    def pair_copy(index, source, target):
+        return remote(source, target, pair_send.at[index], pair_recv.at[index], sibling)
+
+    barrier = pltpu.get_barrier_semaphore()
+    for other in others:
+        pl.semaphore_signal(barrier, inc=1, device_id={AXIS: other}, device_id_type=MESH)
+    loads = [
+        pltpu.make_async_copy(source, target, local_sem.at[i])
+        for i, (source, target) in enumerate(
+            [
+                (offsets_hbm, offsets_ref),
+                (owners_hbm, owners_ref),
+                (grad_hbm, grad_ref),
+                (left_root_hbm, left_root_ref),
+                (right_root_hbm, right_root_ref),
+                (left_hbm, left_ref),
+                (right_hbm, right_ref),
+            ]
+        )
+    ]
+    for load in loads[:5]:
+        load.start()
+
+    loads[0].wait()
+    loads[1].wait()
+    owners = [owners_ref[b] for b in range(n)]
+    offsets = [offsets_ref[b] for b in range(n)]
+    pairs = [owner >> 1 for owner in owners]
+    for k in range(pair_count):
+        first = offsets[0]
+        last = offsets[0]
+        for b in range(1, n):
+            last = jnp.where(pairs[b] == k, offsets[b], last)
+        for b in range(n - 1, -1, -1):
+            first = jnp.where(pairs[b] == k, offsets[b], first)
+        table_ref[2 * k] = first
+        table_ref[2 * k + 1] = last
+    first_owner = owners[0]
+    last_owner = owners[0]
+    for b in range(1, n):
+        last_owner = jnp.where(pairs[b] == pair, owners[b], last_owner)
+    for b in range(n - 1, -1, -1):
+        first_owner = jnp.where(pairs[b] == pair, owners[b], first_owner)
+    first_side = first_owner & 1
+    last_side = last_owner & 1
+    last_rank = jnp.where(first_owner == last_owner, 1, 0)
+    my_side = jnp.where(side == 0, first_side, last_side)
+    my_rank = jnp.where(side == 0, 0, last_rank)
+    sibling_rank = jnp.where(side == 0, last_rank, 0)
+    own_root = my_side == side
+
+    loads[2].wait()
+    squares = jnp.zeros((strip, block_size), jnp.float32)
+    for b in range(n):
+        wide = grad_ref[b].astype(jnp.float32)
+        squares += wide * wide
+    partial = squares[0:8]
+    for r in range(8, strip, 8):
+        partial += squares[r : r + 8]
+    lanes = partial[:, 0:128]
+    for c in range(128, block_size, 128):
+        lanes += partial[:, c : c + 128]
+    sums_ref[me] = lanes
+    pl.semaphore_wait(barrier, n - 1)
+
+    def send_strip(other):
+        outgoing_ref[other] = grad_ref[table_ref[other]]
+        strip_copy(me, other).start()
+
+    for other in to_first:
+        send_strip(other)
+    for other in others:
+        sum_copy(me, other).start()
+    send_strip(sibling)
+    for other in to_last:
+        send_strip(other)
+    blocks_ref[side, rows_of(me)] = grad_ref[table_ref[me]]
+
+    loads[3].wait()
+    root_out_ref[0] = left_root_ref[sibling_rank]
+    left_swap = pair_copy(0, root_out_ref.at[0], root_in_ref.at[0])
+    left_swap.start()
+    loads[4].wait()
+    root_out_ref[1] = right_root_ref[sibling_rank]
+    right_swap = pair_copy(1, root_out_ref.at[1], root_in_ref.at[1])
+    right_swap.start()
+    loads[5].start()
+    loads[6].start()
+
+    for other in others:
+        sum_copy(other, me).wait_recv()
+    total = jnp.sum(jnp.sum(sums_ref[...], axis=0), axis=(0, 1), keepdims=True)
+    clip_factor = jnp.minimum(1.0, CLIP_RMS * lax.rsqrt(total / (n * block_size * block_size)))
+    left_swap.wait_recv()
+    right_swap.wait_recv()
+    root_ref[0] = jnp.where(own_root, left_root_ref[my_rank], root_in_ref[0])
+    root_ref[1] = jnp.where(own_root, right_root_ref[my_rank], root_in_ref[1])
+
+    for other in others:
+        strip_copy(other, me).wait_recv()
+    block_swap = pair_copy(2, blocks_ref.at[side], blocks_ref.at[side])
+    block_swap.start()
+
+    block = blocks_ref[side]
+    grad_mean = mean_square(block.astype(jnp.float32))
+    left_half = jnp.dot(root_ref[0], block, preferred_element_type=jnp.float32)
+    direction = jnp.dot(
+        left_half.astype(jnp.bfloat16),
+        root_ref[1],
+        preferred_element_type=jnp.float32,
+    )
+    graft_scale = jnp.sqrt(grad_mean / (mean_square(direction) + EPSILON))
+    slot_update_ref[...] = (clip_factor * (graft_scale * direction)).astype(jnp.bfloat16)
+    for other in others:
+        back_copy(me, other).start()
+    returned_ref[me] = slot_update_ref[rows_of(me)]
+
+    for p in range(n):
+        holder = 0
+        for d in range(n):
+            holder = jnp.where(table_ref[d] == p, d, holder)
+        place_ref[p] = holder
+
+    loads[5].wait()
+    loads[6].wait()
+    pair_copy(2, blocks_ref.at[1 - side], blocks_ref.at[1 - side]).wait_recv()
+    stores = []
+    for s in range(capacity):
+        from_first = (first_side == side) & (s == 0)
+        from_last = (last_side == side) & (last_rank == s)
+        index = jnp.where(from_last, 1, 0)
+        filled = jnp.where(from_first | from_last, 1.0, 0.0).astype(jnp.bfloat16)
+        slot_grad_ref[s] = blocks_ref[index] * filled
+        for ref, out, axis in ((left_ref, left_out, 1), (right_ref, right_out, 0)):
+            product = lax.dot_general(
+                slot_grad_ref[s],
+                slot_grad_ref[s],
+                (((axis,), (axis,)), ((), ())),
+                preferred_element_type=jnp.float32,
+            )
+            ref[s] = DECAY * ref[s] + (1.0 - DECAY) * product
+            store = pltpu.make_async_copy(ref.at[s], out.at[s], stat_sem.at[len(stores)])
+            store.start()
+            stores.append(store)
+
+    for copy in [left_swap, right_swap, block_swap]:
+        copy.wait_send()
+    for other in others:
+        strip_copy(me, other).wait_send()
+        sum_copy(me, other).wait_send()
+    for store in stores:
+        store.wait()
+    for other in others:
+        back_copy(other, me).wait_recv()
+    for p in range(n):
+        update_ref[p] = returned_ref[place_ref[p]]
+    for other in others:
+        back_copy(me, other).wait_send()
+
+
+def exchange(n, grad_shards, offsets, owners, left_stats, right_stats, left_root, right_root):
+    blocks, strip, size = grad_shards.shape
+    capacity = left_root.shape[0]
+    half = jnp.bfloat16
+    anywhere = pl.BlockSpec(memory_space=pl.ANY)
+    many = pltpu.SemaphoreType.DMA((n,))
+    operands = [
+        pltpu.with_memory_space_constraint(array, pltpu.HBM)
+        for array in (
+            offsets,
+            owners,
+            grad_shards,
+            left_stats,
+            right_stats,
+            left_root,
+            right_root,
+        )
+    ]
+    return pl.pallas_call(
+        functools.partial(exchange_kernel, n),
+        out_shape=(
+            jax.ShapeDtypeStruct((n, strip, size), half),
+            jax.ShapeDtypeStruct(left_stats.shape, jnp.float32),
+            jax.ShapeDtypeStruct(right_stats.shape, jnp.float32),
+        ),
+        in_specs=[anywhere] * len(operands),
+        out_specs=(pl.BlockSpec(memory_space=pltpu.VMEM), anywhere, anywhere),
+        scratch_shapes=[
+            pltpu.SMEM((n,), jnp.int32),
+            pltpu.SMEM((n,), jnp.int32),
+            pltpu.SMEM((n,), jnp.int32),
+            pltpu.SMEM((n,), jnp.int32),
+            pltpu.VMEM((blocks, strip, size), half),
+            pltpu.VMEM((n, strip, size), half),
+            pltpu.VMEM((2, size, size), half),
+            pltpu.VMEM((capacity, size, size), half),
+            pltpu.VMEM((capacity, size, size), half),
+            pltpu.VMEM((2, size, size), half),
+            pltpu.VMEM((2, size, size), half),
+            pltpu.VMEM((2, size, size), half),
+            pltpu.VMEM((size, size), half),
+            pltpu.VMEM((n, strip, size), half),
+            pltpu.VMEM((capacity, size, size), half),
+            pltpu.VMEM((capacity, size, size), jnp.float32),
+            pltpu.VMEM((capacity, size, size), jnp.float32),
+            pltpu.VMEM((n, 8, 128), jnp.float32),
+            pltpu.SemaphoreType.DMA((len(operands),)),
+            pltpu.SemaphoreType.DMA((2 * capacity,)),
+            many,
+            many,
+            many,
+            many,
+            many,
+            many,
+            pltpu.SemaphoreType.DMA((3,)),
+            pltpu.SemaphoreType.DMA((3,)),
+        ],
+        compiler_params=pltpu.CompilerParams(
+            collective_id=0, has_side_effects=True, vmem_limit_bytes=32 * 1024 * 1024
+        ),
+        cost_estimate=pl.CostEstimate(
+            flops=4 * (1 + capacity) * size**3,
+            bytes_accessed=32 * 1024 * 1024,
+            transcendentals=0,
+        ),
+        name="exchange",
+    )(*operands)
+
+
+def store_kernel(*refs):
+    count = (len(refs) - 1) // 2
+    sources, targets, sems = refs[:count], refs[count : 2 * count], refs[-1]
+    copies = []
+    for source, target in zip(sources, targets):
+        pieces = 4
+        size = source.shape[0] * source.shape[1] // pieces
+        for piece in range(pieces):
+            if source.shape[0] >= pieces:
+                step = source.shape[0] // pieces
+                part = pl.ds(piece * step, step)
+                pair = (source.at[part], target.at[part])
+            else:
+                index, row = divmod(piece * size, source.shape[1])
+                part = pl.ds(row, size)
+                pair = (source.at[index, part], target.at[index, part])
+            copy = pltpu.make_async_copy(*pair, sems.at[len(copies)])
+            copy.start()
+            copies.append(copy)
+    for copy in copies:
+        copy.wait()
+
+
+def store(*arrays):
+    anywhere = pl.BlockSpec(memory_space=pl.ANY)
+    return pl.pallas_call(
+        store_kernel,
+        out_shape=tuple(jax.ShapeDtypeStruct(a.shape, a.dtype) for a in arrays),
+        in_specs=[pl.BlockSpec(memory_space=pltpu.VMEM)] * len(arrays),
+        out_specs=(anywhere,) * len(arrays),
+        scratch_shapes=[pltpu.SemaphoreType.DMA((4 * len(arrays),))],
+        compiler_params=pltpu.CompilerParams(vmem_limit_bytes=16 * 1024 * 1024),
+        name="store",
+    )(*arrays)
+
+
+def body(grad_shards, offsets, owners, left_stats, right_stats, left_root, right_root):
+    n = lax.axis_size(AXIS)
+    blocks, strip, _ = grad_shards.shape
+    if blocks != n or strip % 16 or left_stats.shape[0] != 2:
+        return padded_body(
+            grad_shards, offsets, owners, left_stats, right_stats, left_root, right_root
+        )
+    return store(
+        *exchange(
+            n, grad_shards, offsets, owners, left_stats, right_stats, left_root, right_root
+        )
+    )
+
+
 def solution(mesh):
     placed = (
         P("groups", "fsdp", None),

time: 109 us -> 35.6 us (0.33); the launches traced: 107 us -> 35.4 us
  blocking collectives: 44.2 us -> 0 us
  Pallas kernels: 0 us -> 34.8 us
  waiting for transfers between devices: 15.8 us -> 0 us
  starting transfers between devices: 11.6 us -> 0 us
  local copies, waits for them, and re-layouts: 11 us -> 0 us
  other arithmetic: 10.4 us -> 0 us
  matrix products: 9.76 us -> 0 us
  between operations: 4.29 us -> 0.64 us
    psum x1 -> x0, blocking collectives: 44.2 us -> none  [body(): square_sum = lax.psum(jnp.sum(local_grad * local_grad), 'fsdp')]
    pallas_call x0 -> x2, Pallas kernels: none -> 34.8 us  [the longest x1 32.5 us: exchange(): pl.pallas_call(functools.partial(exchange_kernel, n), out_shape=(jax.Shap...]
    all_to_all x2 -> x0, waiting for transfers between devices: 15.8 us -> none  [the longest x1 15.8 us: body(): lax.all_to_all(slot_updates, 'fsdp', split_axis=1, concat_axis=1, tiled=T...]
    all_to_all x2 -> x0, starting transfers between devices: 11.6 us -> none  [the longest x1 7.32 us: body(): lax.all_to_all(outgoing, 'fsdp', split_axis=1, concat_axis=1, tiled=True)]
    dot_general x6 -> x0, matrix products: 9.76 us -> none  [the longest x2 6.48 us: precondition(): jnp.dot(left_half, right_inv, preferred_element_type=jnp.float32)]
    reduce_sum x5 -> x0, other arithmetic: 4.97 us -> none  [the longest x1 2.27 us: body(): slot_squares = jnp.sum(widened * widened, axis=(1, 2))]
    another operation x5 -> x0, other arithmetic: 3.39 us -> none  [the longest x2 3.03 us: body(): return (update, jnp.stack(left_list), jnp.stack(right_list))]
    gather x2 -> x0, local copies, waits for them, and re-layouts: 2.24 us -> none  [the longest x1 1.66 us: body(): picked = jnp.take(grad_shards, source_rows, axis=0)]
  transfers between devices with their start and end apart: 2 -> 0, of which waited for: 1 -> 0; matrix products, arithmetic and copies ran while one was open for 7% -> 0% of each run, Pallas kernels for 0% -> 0%
where the time goes in v2:
time: 35.6 us; the launch traced here: 35.4 us
  Pallas kernels  34.8 us (98%)
  between operations  0.64 us (2%)
    pallas_call x1, Pallas kernels, exchange(): pl.pallas_call(functools.partial(exchange_kernel, n), out_shape=(jax.Shap...  32.5 us
    pallas_call x1, Pallas kernels, store(): pl.pallas_call(store_kernel, out_shape=tuple((jax.ShapeDtypeStruct(a.shap...  2.28 us

profile of v2, /device:TPU:1, one launch (start us, length us, event | category | flops | bytes accessed | tf_op | source)
XLA Modules:
  0.0 35.4 jit_solution(15691533720633480508)
XLA Ops:
  0.6 32.5 %exchange.1 = (bf16[16,32,512]{2,1,0:T(8,128)(2,1)S(1)}, f32[2,512,512]{2,1,0:T(8,128)S(1)}, f32[2,512,512]{2,1,0:T(8,128)S(1)}) custom-call(s32[16]{0:T(128)} %offsets_hbm.1, s32[16]{0:T(128)} %owners_hbm.1, bf16[16,32,512]{2,1,0:T(8,128)(2,1)} %grad_hbm.1, f32[2,512,512]{2,1,0:T(8,128)} %left_hbm.1, f32[2,512,512]{2,1,0:T(8,128)} %right_hbm.1, ...), custom_call_target="tpu_custom_call" | custom-call | flops 1610612736 | bytes 33554432 | tf_op jit(solution)/shard_map/exchange/pallas_call | solution.py:369
  33.2 2.3 %store.1 = (bf16[16,32,512]{2,1,0:T(8,128)(2,1)}, f32[2,512,512]{2,1,0:T(8,128)}, f32[2,512,512]{2,1,0:T(8,128)}) custom-call(bf16[16,32,512]{2,1,0:T(8,128)(2,1)S(1)} %get-tuple-element.6.refs_0_, f32[2,512,512]{2,1,0:T(8,128)S(1)} %get-tuple-element.7.refs_1_, f32[2,512,512]{2,1,0:T(8,128)S(1)} %get-tuple-element.8.refs_2_), custom_call_target="tpu_custom_call" | custom-call | tf_op jit(solution)/shard_map/store/pallas_call | solution.py:445

commit v3 on v2

--- a/solution.py
+++ b/solution.py
@@ -120,7 +120,6 @@
     root_ref,
     slot_update_ref,
     returned_ref,
-    slot_grad_ref,
     left_ref,
     right_ref,
     sums_ref,
@@ -148,7 +147,7 @@
         return jnp.where(ahead >= pair_count, ahead - pair_count, ahead)
 
     middle = pair_count // 2
-    steps = sorted(range(1, pair_count), key=lambda k: (abs(k - middle), k))
+    steps = sorted(range(1, pair_count), key=lambda k: k)
     to_first = [2 * wrapped(k) for k in steps]
     to_last = [2 * wrapped(k) + 1 for k in steps]
     others = to_first + to_last + [sibling]
@@ -240,6 +239,14 @@
     own_root = my_side == side
 
     loads[2].wait()
+    pl.semaphore_wait(barrier, n - 1)
+
+    def send_strip(other):
+        outgoing_ref[other] = grad_ref[table_ref[other]]
+        strip_copy(me, other).start()
+
+    for other in to_first:
+        send_strip(other)
     squares = jnp.zeros((strip, block_size), jnp.float32)
     for b in range(n):
         wide = grad_ref[b].astype(jnp.float32)
@@ -251,14 +258,6 @@
     for c in range(128, block_size, 128):
         lanes += partial[:, c : c + 128]
     sums_ref[me] = lanes
-    pl.semaphore_wait(barrier, n - 1)
-
-    def send_strip(other):
-        outgoing_ref[other] = grad_ref[table_ref[other]]
-        strip_copy(me, other).start()
-
-    for other in to_first:
-        send_strip(other)
     for other in others:
         sum_copy(me, other).start()
     send_strip(sibling)
@@ -286,14 +285,66 @@
     root_ref[0] = jnp.where(own_root, left_root_ref[my_rank], root_in_ref[0])
     root_ref[1] = jnp.where(own_root, right_root_ref[my_rank], root_in_ref[1])
 
-    for other in others:
-        strip_copy(other, me).wait_recv()
+    swapped = pair_copy(2, blocks_ref.at[1 - side], blocks_ref.at[1 - side])
+    stats = ((left_ref, left_out, 1), (right_ref, right_out, 0))
+    stores = []
+
+    def product(index, axis):
+        return (1.0 - DECAY) * lax.dot_general(
+            blocks_ref[index],
+            blocks_ref[index],
+            (((axis,), (axis,)), ((), ())),
+            preferred_element_type=jnp.float32,
+        )
+
+    def add_first():
+        loads[5].wait()
+        loads[6].wait()
+        for ref, _, axis in stats:
+            ref[0] = DECAY * ref[0] + jnp.where(first_side == side, product(0, axis), 0.0)
+
+    def add_last():
+        for ref, out, axis in stats:
+            change = product(1, axis)
+            for s in range(capacity):
+                old = ref[s] if s == 0 else DECAY * ref[s]
+                here = (last_side == side) & (last_rank == s)
+                ref[s] = old + jnp.where(here, change, 0.0)
+                store = pltpu.make_async_copy(ref.at[s], out.at[s], stat_sem.at[len(stores)])
+                store.start()
+                stores.append(store)
+
+    @pl.when(side == 1)
+    def _():
+        swapped.wait_recv()
+        add_first()
+
+    half = n // 2
+    near = me // half
+    far = 1 - near
+
+    def partial_half(part):
+        span = pl.ds(pl.multiple_of(part * (block_size // 2), block_size // 2), block_size // 2)
+        rows = blocks_ref[side, span]
+        wide = rows.astype(jnp.float32)
+        squares = jnp.sum(wide * wide, axis=(0, 1), keepdims=True)
+        product = jnp.dot(root_ref[0, :, span], rows, preferred_element_type=jnp.float32)
+        return squares, product
+
+    offset = me - near * half
+    for k in range(1, half):
+        ahead = offset + k
+        ahead = jnp.where(ahead >= half, ahead - half, ahead)
+        strip_copy(near * half + ahead, me).wait_recv()
+    near_squares, near_product = partial_half(near)
+    for k in range(half):
+        strip_copy(far * half + k, me).wait_recv()
     block_swap = pair_copy(2, blocks_ref.at[side], blocks_ref.at[side])
     block_swap.start()
 
-    block = blocks_ref[side]
-    grad_mean = mean_square(block.astype(jnp.float32))
-    left_half = jnp.dot(root_ref[0], block, preferred_element_type=jnp.float32)
+    far_squares, far_product = partial_half(far)
+    grad_mean = (near_squares + far_squares) / (block_size * block_size)
+    left_half = near_product + far_product
     direction = jnp.dot(
         left_half.astype(jnp.bfloat16),
         root_ref[1],
@@ -301,8 +352,10 @@
     )
     graft_scale = jnp.sqrt(grad_mean / (mean_square(direction) + EPSILON))
     slot_update_ref[...] = (clip_factor * (graft_scale * direction)).astype(jnp.bfloat16)
-    for other in others:
-        back_copy(me, other).start()
+    for a, b in zip(to_first, to_last):
+        back_copy(me, a).start()
+        back_copy(me, b).start()
+    back_copy(me, sibling).start()
     returned_ref[me] = slot_update_ref[rows_of(me)]
 
     for p in range(n):
@@ -311,35 +364,19 @@
             holder = jnp.where(table_ref[d] == p, d, holder)
         place_ref[p] = holder
 
-    loads[5].wait()
-    loads[6].wait()
-    pair_copy(2, blocks_ref.at[1 - side], blocks_ref.at[1 - side]).wait_recv()
-    stores = []
-    for s in range(capacity):
-        from_first = (first_side == side) & (s == 0)
-        from_last = (last_side == side) & (last_rank == s)
-        index = jnp.where(from_last, 1, 0)
-        filled = jnp.where(from_first | from_last, 1.0, 0.0).astype(jnp.bfloat16)
-        slot_grad_ref[s] = blocks_ref[index] * filled
-        for ref, out, axis in ((left_ref, left_out, 1), (right_ref, right_out, 0)):
-            product = lax.dot_general(
-                slot_grad_ref[s],
-                slot_grad_ref[s],
-                (((axis,), (axis,)), ((), ())),
-                preferred_element_type=jnp.float32,
-            )
-            ref[s] = DECAY * ref[s] + (1.0 - DECAY) * product
-            store = pltpu.make_async_copy(ref.at[s], out.at[s], stat_sem.at[len(stores)])
-            store.start()
-            stores.append(store)
-
+    @pl.when(side == 0)
+    def _():
+        add_first()
+        swapped.wait_recv()
+
+    add_last()
     for copy in [left_swap, right_swap, block_swap]:
         copy.wait_send()
     for other in others:
         strip_copy(me, other).wait_send()
         sum_copy(me, other).wait_send()
-    for store in stores:
-        store.wait()
+    for copy in stores:
+        copy.wait()
     for other in others:
         back_copy(other, me).wait_recv()
     for p in range(n):
@@ -390,7 +427,6 @@
             pltpu.VMEM((2, size, size), half),
             pltpu.VMEM((size, size), half),
             pltpu.VMEM((n, strip, size), half),
-            pltpu.VMEM((capacity, size, size), half),
             pltpu.VMEM((capacity, size, size), jnp.float32),
             pltpu.VMEM((capacity, size, size), jnp.float32),
             pltpu.VMEM((n, 8, 128), jnp.float32),

time: 35.6 us -> 33.9 us (0.952)
  the two profiles are of different devices: /device:TPU:1 before, /device:TPU:25 now
where the time goes in v3:
time: 33.9 us; the launch traced here: 33.7 us
  Pallas kernels  33.1 us (98%)
  between operations  0.64 us (2%)
    pallas_call x1, Pallas kernels, exchange(): pl.pallas_call(functools.partial(exchange_kernel, n), out_shape=(jax.Shap...  30.8 us
    pallas_call x1, Pallas kernels, store(): pl.pallas_call(store_kernel, out_shape=tuple((jax.ShapeDtypeStruct(a.shap...  2.28 us

profile of v3, /device:TPU:25, one launch (start us, length us, event | category | flops | bytes accessed | tf_op | source)
XLA Modules:
  0.0 33.7 jit_solution(7697937898948308655)
XLA Ops:
  0.6 30.8 %exchange.1 = (bf16[16,32,512]{2,1,0:T(8,128)(2,1)S(1)}, f32[2,512,512]{2,1,0:T(8,128)S(1)}, f32[2,512,512]{2,1,0:T(8,128)S(1)}) custom-call(s32[16]{0:T(128)} %offsets_hbm.1, s32[16]{0:T(128)} %owners_hbm.1, bf16[16,32,512]{2,1,0:T(8,128)(2,1)} %grad_hbm.1, f32[2,512,512]{2,1,0:T(8,128)} %left_hbm.1, f32[2,512,512]{2,1,0:T(8,128)} %right_hbm.1, ...), custom_call_target="tpu_custom_call" | custom-call | flops 1610612736 | bytes 33554432 | tf_op jit(solution)/shard_map/exchange/pallas_call | solution.py:406
  31.5 2.3 %store.1 = (bf16[16,32,512]{2,1,0:T(8,128)(2,1)}, f32[2,512,512]{2,1,0:T(8,128)}, f32[2,512,512]{2,1,0:T(8,128)}) custom-call(bf16[16,32,512]{2,1,0:T(8,128)(2,1)S(1)} %get-tuple-element.6.refs_0_, f32[2,512,512]{2,1,0:T(8,128)S(1)} %get-tuple-element.7.refs_1_, f32[2,512,512]{2,1,0:T(8,128)S(1)} %get-tuple-element.8.refs_2_), custom_call_target="tpu_custom_call" | custom-call | tf_op jit(solution)/shard_map/store/pallas_call | solution.py:481

commit v4 on v3

--- a/solution.py
+++ b/solution.py
@@ -191,8 +191,6 @@
         return remote(source, target, pair_send.at[index], pair_recv.at[index], sibling)
 
     barrier = pltpu.get_barrier_semaphore()
-    for other in others:
-        pl.semaphore_signal(barrier, inc=1, device_id={AXIS: other}, device_id_type=MESH)
     loads = [
         pltpu.make_async_copy(source, target, local_sem.at[i])
         for i, (source, target) in enumerate(
@@ -207,7 +205,11 @@
             ]
         )
     ]
-    for load in loads[:5]:
+    for load in loads[:3]:
+        load.start()
+    for other in others:
+        pl.semaphore_signal(barrier, inc=1, device_id={AXIS: other}, device_id_type=MESH)
+    for load in loads[3:5]:
         load.start()
 
     loads[0].wait()
@@ -458,7 +460,7 @@
     sources, targets, sems = refs[:count], refs[count : 2 * count], refs[-1]
     copies = []
     for source, target in zip(sources, targets):
-        pieces = 4
+        pieces = 2
         size = source.shape[0] * source.shape[1] // pieces
         for piece in range(pieces):
             if source.shape[0] >= pieces:
@@ -483,7 +485,7 @@
         out_shape=tuple(jax.ShapeDtypeStruct(a.shape, a.dtype) for a in arrays),
         in_specs=[pl.BlockSpec(memory_space=pltpu.VMEM)] * len(arrays),
         out_specs=(anywhere,) * len(arrays),
-        scratch_shapes=[pltpu.SemaphoreType.DMA((4 * len(arrays),))],
+        scratch_shapes=[pltpu.SemaphoreType.DMA((2 * len(arrays),))],
         compiler_params=pltpu.CompilerParams(vmem_limit_bytes=16 * 1024 * 1024),
         name="store",
     )(*arrays)

time: 33.9 us -> 33.8 us (level)
  no operation moved by 1% of the time
where the time goes in v4:
time: 33.8 us; the launch traced here: 33.7 us
  Pallas kernels  33.1 us (98%)
  between operations  0.64 us (2%)
    pallas_call x1, Pallas kernels, exchange(): pl.pallas_call(functools.partial(exchange_kernel, n), out_shape=(jax.Shap...  30.8 us
    pallas_call x1, Pallas kernels, store(): pl.pallas_call(store_kernel, out_shape=tuple((jax.ShapeDtypeStruct(a.shap...  2.23 us

profile of v4, /device:TPU:25, one launch (start us, length us, event | category | flops | bytes accessed | tf_op | source)
XLA Modules:
  0.0 33.7 jit_solution(11549116055553714664)
XLA Ops:
  0.6 30.8 %exchange.1 = (bf16[16,32,512]{2,1,0:T(8,128)(2,1)S(1)}, f32[2,512,512]{2,1,0:T(8,128)S(1)}, f32[2,512,512]{2,1,0:T(8,128)S(1)}) custom-call(s32[16]{0:T(128)} %offsets_hbm.1, s32[16]{0:T(128)} %owners_hbm.1, bf16[16,32,512]{2,1,0:T(8,128)(2,1)} %grad_hbm.1, f32[2,512,512]{2,1,0:T(8,128)} %left_hbm.1, f32[2,512,512]{2,1,0:T(8,128)} %right_hbm.1, ...), custom_call_target="tpu_custom_call" | custom-call | flops 1610612736 | bytes 33554432 | tf_op jit(solution)/shard_map/exchange/pallas_call | solution.py:408
  31.5 2.2 %store.1 = (bf16[16,32,512]{2,1,0:T(8,128)(2,1)}, f32[2,512,512]{2,1,0:T(8,128)}, f32[2,512,512]{2,1,0:T(8,128)}) custom-call(bf16[16,32,512]{2,1,0:T(8,128)(2,1)S(1)} %get-tuple-element.6.refs_0_, f32[2,512,512]{2,1,0:T(8,128)S(1)} %get-tuple-element.7.refs_1_, f32[2,512,512]{2,1,0:T(8,128)S(1)} %get-tuple-element.8.refs_2_), custom_call_target="tpu_custom_call" | custom-call | tf_op jit(solution)/shard_map/store/pallas_call | solution.py:483
